TPU v7x, 32 devices: a whole 2x2x4 slice. The times are simulated.
32 devices in a mesh: src: 4 (over y, core), tgt: 8 (over z, x).
Axes of the slice: x: 2, y: 2, z: 4, core: 2. Of those that a mesh axis runs over, the one named last changes fastest.
Arguments:
- noise: float32 [4096, 384], P(('src', 'tgt')), may hold values from -16 to 16
- data: float32 [8192, 384], P('tgt', 'src'), may hold values from -6 to 6
Outputs:
- velocity: float32 [4096, 384], P(('src', 'tgt'))
- target_potential: float32 [8192], P('tgt')
All inputs are finite; a program needn't handle non-finite values.
Results may differ from a plain program's by a relative error of at most 0.0003.
Values sent between devices are 32-bit elements; how exact they have to be, the bound alone decides.
A program may use at most 64 MiB of HBM per device.

v0:
```python
import math

import jax
import jax.numpy as jnp
from jax import lax
from jax.sharding import PartitionSpec as P

ITERS = 3


EPS = 0.05


def row_merge(z_tile):
    local_top = jnp.max(z_tile, axis=1)
    top = lax.pmax(local_top, "tgt")
    total = lax.psum(jnp.sum(jnp.exp(z_tile - top[:, None]), axis=1), "tgt")
    return top + jnp.log(total)


def col_merge(z_tile):
    local_top = jnp.max(z_tile, axis=0)
    top = lax.pmax(local_top, "src")
    total = lax.psum(jnp.sum(jnp.exp(z_tile - top[None, :]), axis=0), "src")
    return top + jnp.log(total)


def per_device(noise, data):
    source_rows = lax.all_gather(noise, "tgt", axis=0, tiled=True)
    target_rows = lax.all_gather(data, "src", axis=1, tiled=True)
    feat_width = source_rows.shape[1]
    src_total = source_rows.shape[0] * lax.axis_size("src")
    tgt_total = target_rows.shape[0] * lax.axis_size("tgt")
    source_sq = jnp.sum(source_rows * source_rows, axis=1)
    target_sq = jnp.sum(target_rows * target_rows, axis=1)
    cross = jnp.dot(
        source_rows,
        target_rows.T,
        precision=lax.Precision.HIGHEST,
        preferred_element_type=jnp.float32,
    )
    cost_tile = (source_sq[:, None] + target_sq[None, :] - 2.0 * cross) / feat_width
    g_pot = jnp.zeros((target_rows.shape[0],), jnp.float32)
    for step_index in range(ITERS):
        f_pot = -EPS * (math.log(src_total) + row_merge((g_pot[None, :] - cost_tile) / EPS))
        g_pot = -EPS * (math.log(tgt_total) + col_merge((f_pot[:, None] - cost_tile) / EPS))
    z_final = (g_pot[None, :] - cost_tile) / EPS
    lrow = row_merge(z_final)
    weight = jnp.exp(z_final - lrow[:, None])
    bary = lax.psum_scatter(
        jnp.dot(
            weight, target_rows, precision=lax.Precision.HIGHEST, preferred_element_type=jnp.float32
        ),
        "tgt",
        scatter_dimension=0,
        tiled=True,
    )
    return (bary - noise, g_pot)


def solution(mesh):
    placed = (P(("src", "tgt"), None), P("tgt", "src"))
    return jax.shard_map(
        per_device,
        mesh=mesh,
        in_specs=placed,
        out_specs=(P(("src", "tgt"), None), P("tgt")),
        check_vma=False,
    )
```

profile of v0, /device:TPU:0, one launch (start us, length us, event | category | flops | bytes accessed | tf_op | source)
XLA Modules:
  0.0 398.1 jit_solution(3295013972332672002)
XLA Ops:
  7.2 0.0 all-gather.5.cloned.1.call-start
  7.2 0.7 all-gather.5.cloned.1.call-update
  7.9 0.0 all-gather.3.cloned.1.call-start
  7.9 0.7 all-gather.3.cloned.1.call-update
  8.6 0.0 reduce-scatter.2.cloned.1.call-start
  8.7 23.3 %all-gather.5.cloned.1.call-done = f32[1024,384]{0,1:T(8,128)} async-done(((f32[1024,96]{0,1:T(8,128)}), f32[1024,384]{0,1:T(8,128)}) %all-gather.5.cloned.1.call-update) | async-done | bytes 1572880 | tf_op jit(solution)/shard_map/all_gather | solution.py:30
  32.0 1.5 multiply_reduce_fusion
  33.5 44.8 %all-gather.3.cloned.1.call-done = f32[1024,384]{1,0:T(8,128)} async-done(((f32[128,384]{1,0:T(8,128)}), f32[1024,384]{1,0:T(8,128)}) %all-gather.3.cloned.1.call-update) | async-done | bytes 1572880 | tf_op jit(solution)/shard_map/all_gather | solution.py:29
  78.3 1.6 multiply_reduce_fusion.1
  80.0 10.5 %fusion.3 = (f32[1024]{0:T(1024)S(1)}, f32[1024,1024]{0,1:T(8,128)}) fusion(f32[1024,384]{1,0:T(8,128)} %all-gather.3.cloned.1.call-done, f32[1024,384]{0,1:T(8,128)} %all-gather.5.cloned.1.call-done, f32[1024]{0:T(1024)S(1)} %multiply_reduce_fusion, f32[1024]{0:T(1024)S(1)} %multiply_reduce_fusion.1), kind=kOutput, calls=%fused_computation.18 | convolution fusion | flops 4839177216 | bytes 7352320 | tf_op jit(solution)/shard_map/dot_general | solution.py:36
  90.5 19.2 %pmax.49 = f32[1024]{0:T(1024)S(1)} all-reduce(f32[1024]{0:T(1024)S(1)} %get-tuple-element.2), channel_id=1, replica_groups=mesh['src'=4,'tgt'=8] {'tgt'}, use_global_device_ids=true, to_apply=%region_3.0 | all-reduce | flops 1024 | bytes 8192 | tf_op jit(solution)/shard_map/pmax | solution.py:16
  109.7 3.0 exponential_reduce_fusion.6
  112.8 17.1 %psum.49 = f32[1024]{0:T(1024)S(1)} all-reduce(f32[1024]{0:T(1024)S(1)} %exponential_reduce_fusion.6), channel_id=1, replica_groups=mesh['src'=4,'tgt'=8] {'tgt'}, use_global_device_ids=true, to_apply=%region_5.0 | all-reduce | flops 1024 | bytes 8192 | tf_op jit(solution)/shard_map/psum | solution.py:17
  129.9 2.7 fusion.4
  132.6 5.7 %pmax.50 = f32[1024]{0:T(1024)S(1)} all-reduce(f32[1024]{0:T(1024)S(1)} %fusion.4), channel_id=1, replica_groups=mesh['src'=4,'tgt'=8] {'src'}, use_global_device_ids=true, to_apply=%region_7.0 | all-reduce | flops 1024 | bytes 8192 | tf_op jit(solution)/shard_map/pmax | solution.py:23
  138.3 3.2 exponential_reduce_fusion.5
  141.4 6.7 %psum.50 = f32[1024]{0:T(1024)S(1)} all-reduce(f32[1024]{0:T(1024)S(1)} %exponential_reduce_fusion.5), channel_id=1, replica_groups=mesh['src'=4,'tgt'=8] {'src'}, use_global_device_ids=true, to_apply=%region_9.0 | all-reduce | flops 1024 | bytes 8192 | tf_op jit(solution)/shard_map/psum | solution.py:24
  148.1 2.7 fusion.5
  150.8 19.1 %pmax.51 = f32[1024]{0:T(1024)S(1)} all-reduce(f32[1024]{0:T(1024)S(1)} %fusion.5), channel_id=1, replica_groups=mesh['src'=4,'tgt'=8] {'tgt'}, use_global_device_ids=true, to_apply=%region_11.0 | all-reduce | flops 1024 | bytes 8192 | tf_op jit(solution)/shard_map/pmax | solution.py:16
  169.9 3.1 exponential_reduce_fusion.4
  173.0 17.2 %psum.51 = f32[1024]{0:T(1024)S(1)} all-reduce(f32[1024]{0:T(1024)S(1)} %exponential_reduce_fusion.4), channel_id=1, replica_groups=mesh['src'=4,'tgt'=8] {'tgt'}, use_global_device_ids=true, to_apply=%region_13.0 | all-reduce | flops 1024 | bytes 8192 | tf_op jit(solution)/shard_map/psum | solution.py:17
  190.2 2.7 fusion.6
  192.8 5.7 %pmax.52 = f32[1024]{0:T(1024)S(1)} all-reduce(f32[1024]{0:T(1024)S(1)} %fusion.6), channel_id=1, replica_groups=mesh['src'=4,'tgt'=8] {'src'}, use_global_device_ids=true, to_apply=%region_15.0 | all-reduce | flops 1024 | bytes 8192 | tf_op jit(solution)/shard_map/pmax | solution.py:23
  198.5 3.2 exponential_reduce_fusion.3
  201.7 6.2 %psum.52 = f32[1024]{0:T(1024)S(1)} all-reduce(f32[1024]{0:T(1024)S(1)} %exponential_reduce_fusion.3), channel_id=1, replica_groups=mesh['src'=4,'tgt'=8] {'src'}, use_global_device_ids=true, to_apply=%region_17.0 | all-reduce | flops 1024 | bytes 8192 | tf_op jit(solution)/shard_map/psum | solution.py:24
  207.9 2.7 fusion.7
  210.6 19.3 %pmax.53 = f32[1024]{0:T(1024)S(1)} all-reduce(f32[1024]{0:T(1024)S(1)} %fusion.7), channel_id=1, replica_groups=mesh['src'=4,'tgt'=8] {'tgt'}, use_global_device_ids=true, to_apply=%region_19.0 | all-reduce | flops 1024 | bytes 8192 | tf_op jit(solution)/shard_map/pmax | solution.py:16
  229.9 3.1 exponential_reduce_fusion.2
  233.0 17.1 %psum.53 = f32[1024]{0:T(1024)S(1)} all-reduce(f32[1024]{0:T(1024)S(1)} %exponential_reduce_fusion.2), channel_id=1, replica_groups=mesh['src'=4,'tgt'=8] {'tgt'}, use_global_device_ids=true, to_apply=%region_21.0 | all-reduce | flops 1024 | bytes 8192 | tf_op jit(solution)/shard_map/psum | solution.py:17
  250.1 2.7 fusion.8
  252.8 5.7 %pmax.54 = f32[1024]{0:T(1024)S(1)} all-reduce(f32[1024]{0:T(1024)S(1)} %fusion.8), channel_id=1, replica_groups=mesh['src'=4,'tgt'=8] {'src'}, use_global_device_ids=true, to_apply=%region_23.0 | all-reduce | flops 1024 | bytes 8192 | tf_op jit(solution)/shard_map/pmax | solution.py:23
  258.5 3.2 exponential_reduce_fusion.1
  261.7 6.6 %psum.54 = f32[1024]{0:T(1024)S(1)} all-reduce(f32[1024]{0:T(1024)S(1)} %exponential_reduce_fusion.1), channel_id=1, replica_groups=mesh['src'=4,'tgt'=8] {'src'}, use_global_device_ids=true, to_apply=%region_25.0 | all-reduce | flops 1024 | bytes 8192 | tf_op jit(solution)/shard_map/psum | solution.py:24
  268.2 0.0 copy-start.2
  268.2 0.0 copy-start
  268.2 2.8 fusion.9
  271.0 19.1 %pmax.55 = f32[1024]{0:T(1024)S(1)} all-reduce(f32[1024]{0:T(1024)S(1)} %fusion.9), channel_id=1, replica_groups=mesh['src'=4,'tgt'=8] {'tgt'}, use_global_device_ids=true, to_apply=%region_27.0 | all-reduce | flops 1024 | bytes 8192 | tf_op jit(solution)/shard_map/pmax | solution.py:16
  290.1 3.1 exponential_reduce_fusion
  293.2 17.2 %psum.55 = f32[1024]{0:T(1024)S(1)} all-reduce(f32[1024]{0:T(1024)S(1)} %exponential_reduce_fusion), channel_id=1, replica_groups=mesh['src'=4,'tgt'=8] {'tgt'}, use_global_device_ids=true, to_apply=%region_29.0 | all-reduce | flops 1024 | bytes 8192 | tf_op jit(solution)/shard_map/psum | solution.py:17
  310.4 0.0 copy-done.2
  310.4 0.0 copy-done
  310.4 0.0 copy-start.1
  310.4 16.4 %fusion = f32[1024,384]{1,0:T(8,128)} fusion(f32[1024,384]{0,1:T(8,128)S(1)} %copy-done, f32[1024,1024]{0,1:T(8,128)} %get-tuple-element.3, f32[1024]{0:T(1024)S(1)} %log_add_fusion, f32[1024]{0:T(1024)S(1)} %add_multiply_fusion), kind=kOutput, calls=%fused_computation | convolution fusion | flops 4834983936 | bytes 7348224 | tf_op jit(solution)/shard_map/dot_general | solution.py:51
  326.9 0.0 reduce-scatter.2.cloned.1.call-update
  326.9 63.1 %reduce-scatter.2.cloned.1.call-done = f32[128,384]{1,0:T(8,128)} async-done(((f32[1024,384]{1,0:T(8,128)}), f32[128,384]{1,0:T(8,128)}) %reduce-scatter.2.cloned.1.call-update) | async-done | bytes 196624 | tf_op jit(solution)/shard_map/reduce_scatter | solution.py:50
  390.0 0.0 copy-done.1
  390.0 1.6 sub.151
  (7 shorter events, 0.1 us)
Async XLA Ops:
  7.2 24.8 %all-gather.5.cloned.1.call-start = ((), (), s32[]{:S(2)}) async-start(), calls=%async_computation.2 | async-start | bytes 1966080 | tf_op jit(solution)/shard_map/all_gather | solution.py:30
  7.9 70.4 %all-gather.3.cloned.1.call-start = ((), (), s32[]{:S(2)}) async-start(), calls=%async_computation.1 | async-start | bytes 1769472 | tf_op jit(solution)/shard_map/all_gather | solution.py:29
  8.6 381.3 %reduce-scatter.2.cloned.1.call-start = ((), (), s32[]{:S(2)}) async-start(), calls=%async_computation.3 | async-start | bytes 1769472 | tf_op jit(solution)/shard_map/reduce_scatter | solution.py:50
  268.2 42.2 %copy-start.2 = (f32[1024]{0:T(1024)}, f32[1024]{0:T(1024)S(1)}, u32[]{:S(2)}) copy-start(f32[1024]{0:T(1024)S(1)} %add_multiply_fusion) | copy-start | bytes 12292
  268.2 42.2 %copy-start = (f32[1024,384]{0,1:T(8,128)S(1)}, f32[1024,384]{0,1:T(8,128)}, u32[]{:S(2)}) copy-start(f32[1024,384]{0,1:T(8,128)} %all-gather.5.cloned.1.call-done) | copy-start | bytes 4718596
  310.4 79.5 %copy-start.1 = (f32[128,384]{1,0:T(8,128)S(1)}, f32[128,384]{1,0:T(8,128)}, u32[]{:S(2)}) copy-start(f32[128,384]{1,0:T(8,128)} %param.2) | copy-start | bytes 589828
Sparse Core Ops, SparseCore 0:
  9.6 22.3 all-gather.4
  34.1 44.1 all-gather.2
  327.0 62.8 reduce-scatter.1
where the time goes:
time: 399 us; the launch traced here: 398 us
  blocking collectives  182 us (46%)
  waiting for transfers between devices  133 us (33%)
  other arithmetic  42.8 us (11%)
  matrix products  27 us (7%)
  between operations  13.9 us (3%)
    pmax x4, blocking collectives, row_merge(): top = lax.pmax(local_top, 'tgt')  76.7 us
    psum x4, blocking collectives, row_merge(): total = lax.psum(jnp.sum(jnp.exp(z_tile - top[:, None]), axis=1), 'tgt')  68.6 us
    reduce_scatter x1, waiting for transfers between devices, per_device(): lax.psum_scatter(jnp.dot(weight, target_rows, precision=lax.Precision.HIG...  63.1 us
    all_gather x1, waiting for transfers between devices, per_device(): source_rows = lax.all_gather(noise, 'tgt', axis=0, tiled=True)  44.8 us
    all_gather x1, waiting for transfers between devices, per_device(): target_rows = lax.all_gather(data, 'src', axis=1, tiled=True)  23.3 us
    psum x3, blocking collectives, col_merge(): total = lax.psum(jnp.sum(jnp.exp(z_tile - top[None, :]), axis=0), 'src')  19.5 us
    pmax x3, blocking collectives, col_merge(): top = lax.pmax(local_top, 'src')  17 us
    dot_general x1, matrix products, per_device(): jnp.dot(weight, target_rows, precision=lax.Precision.HIGHEST, preferred_e...  16.4 us
  transfers between devices with their start and end apart: 3, of which 3 were waited for; matrix products, arithmetic and copies ran while one was open for 0% of the time, Pallas kernels for 0%

commit v1 on v0

v1 whole, which is shorter than its diff:
```python
import functools
import math

import jax
import jax.numpy as jnp
from jax import lax
from jax.experimental import pallas as pl
from jax.experimental.pallas import tpu as pltpu
from jax.sharding import PartitionSpec as P

ITERS = 3
EPS = 0.05
LOG2E = 1.0 / math.log(2.0)
LANES = 128
MESH = pl.DeviceIdType.MESH


def split(value):
    high = value.astype(jnp.bfloat16)
    return high, (value - high.astype(jnp.float32)).astype(jnp.bfloat16)


def kernel(n_s, n_t, noise_ref, data_ref, vel_ref, pot_ref, src_all, tgt_all, tgt_hi, tgt_lo, tile, col, bary,
           row_pair, col_pair, row_sum, col_sum, from_x, to_z, from_z,
           src_ss, src_rs, src_fs, src_fr, tgt_ss, tgt_rs, tgt_fs, tgt_fr,
           rp_s, rp_r, cp_s, cp_r, rs_s, rs_r, cs_s, cs_r, ax_s, ax_r, bz_s, bz_r):
    s_me, t_me = lax.axis_index("src"), lax.axis_index("tgt")
    rows_own, feat = noise_ref.shape
    feat_own = data_ref.shape[1]
    n_rows, n_cols = tile.shape
    row_chunks, col_chunks = n_rows // LANES, n_cols // LANES
    src_total, tgt_total = n_rows * n_s, n_cols * n_t
    halves_t = n_t // 2
    f32 = jnp.float32

    def on_tgt(peer):
        return (s_me, peer)

    def on_src(peer):
        return (peer, t_me)

    barrier = pltpu.get_barrier_semaphore()
    for off in range(1, n_t):
        pl.semaphore_signal(barrier, 1, device_id=on_tgt(lax.rem(t_me + off, n_t)), device_id_type=MESH)
    for off in range(1, n_s):
        pl.semaphore_signal(barrier, 1, device_id=on_src(lax.rem(s_me + off, n_s)), device_id_type=MESH)
    tgt_all[pl.ds(pl.multiple_of(s_me * feat_own, 8), feat_own), :] = data_ref[...].T
    src_all[pl.ds(pl.multiple_of(t_me * rows_own, 8), rows_own), :] = noise_ref[...]
    pl.semaphore_wait(barrier, n_t + n_s - 2)

    def remote(ref, where, dst, send, recv, dev):
        return pltpu.make_async_remote_copy(
            src_ref=ref.at[where], dst_ref=dst, send_sem=send, recv_sem=recv, device_id=dev, device_id_type=MESH)

    def gather_ops(buf, rows, n, me, dev_of, ss, rs, fs, fr):
        hi, lo = me // 2, lax.rem(me, 2)
        nh = n // 2

        def block(idx):
            return buf.at[pl.ds(pl.multiple_of(idx * rows, 8), rows), :]

        def far(h, owner):
            return pltpu.make_async_remote_copy(
                src_ref=block(owner), dst_ref=block(owner), send_sem=ss.at[h], recv_sem=rs.at[owner // 2],
                device_id=dev_of(h * 2 + lo), device_id_type=MESH)

        def near(owner, h):
            return pltpu.make_async_remote_copy(
                src_ref=block(owner), dst_ref=block(owner), send_sem=fs.at[h], recv_sem=fr.at[h],
                device_id=dev_of(hi * 2 + 1 - lo), device_id_type=MESH)

        offs = list(range(1, nh))

        def begin():
            for off in offs:
                far(lax.rem(hi + off, nh), me).start()
            near(me, hi).start()

        def forward():
            for off in offs:
                h = lax.rem(hi + off, nh)
                far(h, h * 2 + lo).wait_recv()
                near(h * 2 + lo, h).start()

        def finish():
            for off in [0] + offs:
                h = lax.rem(hi + off, nh)
                near(h * 2 + 1 - lo, h).wait_recv()

        def drain():
            for off in offs:
                far(lax.rem(hi + off, nh), me).wait_send()
            for off in [0] + offs:
                h = lax.rem(hi + off, nh)
                near(h * 2 + lo, h).wait_send()

        return begin, forward, finish, drain

    g_src = gather_ops(src_all, rows_own, n_t, t_me, on_tgt, src_ss, src_rs, src_fs, src_fr)
    g_tgt = gather_ops(tgt_all, feat_own, n_s, s_me, on_src, tgt_ss, tgt_rs, tgt_fs, tgt_fr)
    g_src[0]()
    g_tgt[0]()
    g_tgt[1]()
    g_src[1]()
    g_tgt[2]()

    def exchange(buf, n, me, dev_of, ss, rs):
        def op(peer, owner):
            return pltpu.make_async_remote_copy(
                src_ref=buf.at[owner], dst_ref=buf.at[owner], send_sem=ss.at[peer], recv_sem=rs.at[owner],
                device_id=dev_of(peer), device_id_type=MESH)

        def start():
            for off in range(1, n):
                op(lax.rem(me + off, n), me).start()

        def wait():
            for off in range(1, n):
                peer = lax.rem(me + off, n)
                op(peer, peer).wait_recv()

        def drain():
            for off in range(1, n):
                op(lax.rem(me + off, n), me).wait_send()

        return start, wait, drain

    x_rp = exchange(row_pair, n_t, t_me, on_tgt, rp_s, rp_r)
    x_cp = exchange(col_pair, n_s, s_me, on_src, cp_s, cp_r)
    x_rs = [exchange(row_sum.at[k], n_t, t_me, on_tgt, rs_s.at[k], rs_r.at[k]) for k in range(ITERS)]
    x_cs = [exchange(col_sum.at[k], n_s, s_me, on_src, cs_s.at[k], cs_r.at[k]) for k in range(ITERS - 1)]

    scale = LOG2E / (feat * EPS)
    t_hi, t_lo = split(tgt_all[...])
    tgt_hi[...] = t_hi
    tgt_lo[...] = t_lo
    g_src[2]()
    source = src_all[...]
    source_sq = jnp.broadcast_to(jnp.sum(source * source, axis=1, keepdims=True), (n_rows, LANES))
    col[...] = source_sq
    s_hi, s_lo = split(source)
    width = 2 * LANES

    def cost_step(k, carry):
        cols = pl.ds(pl.multiple_of(k * width, width), width)
        w_hi, w_lo = tgt_hi[:, cols], tgt_lo[:, cols]
        cross = jnp.dot(s_hi, w_hi, preferred_element_type=f32)
        cross += jnp.dot(s_hi, w_lo, preferred_element_type=f32)
        cross += jnp.dot(s_lo, w_hi, preferred_element_type=f32)
        block = tgt_all[:, cols]
        target_sq = jnp.sum(block * block, axis=0, keepdims=True)
        both = jnp.concatenate([col[...], col[...]], axis=1)
        tile[:, cols] = (both + target_sq - 2.0 * cross) * scale
        return carry

    lax.fori_loop(0, n_cols // width, cost_step, 0)

    def rows_of(c):
        return slice(c * LANES, (c + 1) * LANES)

    for c in range(row_chunks):
        top = -tile[rows_of(c), rows_of(0)]
        for k in range(1, col_chunks):
            top = jnp.maximum(top, -tile[rows_of(c), rows_of(k)])
        total = jnp.zeros_like(top)
        for k in range(col_chunks):
            total += jnp.exp2(-tile[rows_of(c), rows_of(k)] - top)
        top, total = top.T, total.T
        best = jnp.max(top, axis=0, keepdims=True)
        row_pair[t_me, c:c + 1, :] = best
        row_pair[t_me, row_chunks + c:row_chunks + c + 1, :] = jnp.sum(
            total * jnp.exp2(top - best), axis=0, keepdims=True)
    x_rp[0]()
    x_rp[1]()

    def merge(buf, n, chunks):
        best = buf[0, :chunks, :]
        for d in range(1, n):
            best = jnp.maximum(best, buf[d, :chunks, :])
        total = jnp.zeros_like(best)
        for d in range(n):
            total += buf[d, chunks:, :] * jnp.exp2(buf[d, :chunks, :] - best)
        return best + jnp.log(total) * LOG2E

    def to_col(packed):
        for c in range(row_chunks):
            col[rows_of(c), :] = jnp.broadcast_to(packed[c:c + 1, :], (LANES, LANES)).T

    f_pot = -(math.log2(src_total) + merge(row_pair, n_t, row_chunks))
    to_col(f_pot)

    tops = []
    for k in range(col_chunks):
        def top_step(c, best, k=k):
            rows = pl.ds(pl.multiple_of(c * LANES, LANES), LANES)
            z = col[rows, :] - tile[rows, rows_of(k)]
            return jnp.maximum(best, jnp.max(z.reshape(LANES // 8, 8, LANES), axis=0))

        best = lax.fori_loop(0, row_chunks, top_step, jnp.full((8, LANES), -jnp.inf, f32), unroll=True)
        best = jnp.max(best, axis=0, keepdims=True)
        tops.append(best)

        def exp_step(c, total, k=k, best=best):
            rows = pl.ds(pl.multiple_of(c * LANES, LANES), LANES)
            e = jnp.exp2(col[rows, :] - tile[rows, rows_of(k)] - best)
            tile[rows, rows_of(k)] = e
            return total + jnp.sum(e.reshape(LANES // 8, 8, LANES), axis=0)

        total = lax.fori_loop(0, row_chunks, exp_step, jnp.zeros((8, LANES), f32), unroll=True)
        col_pair[s_me, k:k + 1, :] = best
        col_pair[s_me, col_chunks + k:col_chunks + k + 1, :] = jnp.sum(total, axis=0, keepdims=True)
    x_cp[0]()
    x_cp[1]()
    g_first = -(math.log2(tgt_total) + merge(col_pair, n_s, col_chunks))
    base = jnp.exp2(jnp.concatenate(tops, axis=0) + g_first)
    b = base

    def row_products(slot, b):
        for c in range(row_chunks):
            total = tile[rows_of(c), rows_of(0)] * b[0:1, :]
            for k in range(1, col_chunks):
                total += tile[rows_of(c), rows_of(k)] * b[k:k + 1, :]
            row_sum[slot, t_me, c:c + 1, :] = jnp.sum(total.T, axis=0, keepdims=True)

    def add_up(buf, slot, n):
        total = buf[slot, 0]
        for d in range(1, n):
            total += buf[slot, d]
        return total

    for it in range(ITERS - 1):
        row_products(it, b)
        x_rs[it][0]()
        x_rs[it][1]()
        to_col(1.0 / (src_total * add_up(row_sum, it, n_t)))
        for k in range(col_chunks):
            total = jnp.zeros((8, LANES), f32)
            for c in range(row_chunks):
                e = tile[rows_of(c), rows_of(k)] * col[rows_of(c), :]
                total += jnp.sum(e.reshape(LANES // 8, 8, LANES), axis=0)
            col_sum[it, s_me, k:k + 1, :] = jnp.sum(total, axis=0, keepdims=True) * base[k:k + 1, :]
        x_cs[it][0]()
        x_cs[it][1]()
        beta = 1.0 / (tgt_total * add_up(col_sum, it, n_s))
        b = base * beta
    pot_ref[...] = EPS * (g_first * math.log(2.0) + jnp.log(beta))

    last = ITERS - 1
    row_products(last, b)
    x_rs[last][0]()
    for k in range(col_chunks):
        t_hi, t_lo = split(tgt_all[:, rows_of(k)] * b[k:k + 1, :])
        tgt_hi[:, rows_of(k)] = t_hi
        tgt_lo[:, rows_of(k)] = t_lo

    h_me, l_me = t_me // 2, lax.rem(t_me, 2)
    pair = 2 * rows_own
    dims = (((1,), (1,)), ((), ()))

    def send_x(h, lo):
        return pltpu.make_async_remote_copy(
            src_ref=bary.at[pl.ds(pl.multiple_of((h * 2 + lo) * rows_own, 8), rows_own), :], dst_ref=from_x.at[h],
            send_sem=ax_s.at[h], recv_sem=ax_r.at[h], device_id=on_tgt(h_me * 2 + 1 - l_me), device_id_type=MESH)

    def send_z(h, sender):
        return pltpu.make_async_remote_copy(
            src_ref=to_z.at[h], dst_ref=from_z.at[sender], send_sem=bz_s.at[h], recv_sem=bz_r.at[sender],
            device_id=on_tgt(h * 2 + l_me), device_id_type=MESH)

    def own_rows(h):
        return bary[pl.ds(pl.multiple_of((h * 2 + l_me) * rows_own, 8), rows_own), :]

    def compute(h):
        rows = pl.ds(pl.multiple_of(h * pair, 16), pair)
        e_hi, e_lo = split(tile[rows, :])
        out = lax.dot_general(e_hi, tgt_hi[...], dims, preferred_element_type=f32)
        out += lax.dot_general(e_hi, tgt_lo[...], dims, preferred_element_type=f32)
        out += lax.dot_general(e_lo, tgt_hi[...], dims, preferred_element_type=f32)
        bary[rows, :] = out
        send_x(h, 1 - l_me).start()

    def pass_on(h):
        send_x(h, 1 - l_me).wait_recv()
        to_z[h] = own_rows(h) + from_x[h]
        send_z(h, h_me).start()

    def step(off, carry):
        compute(lax.rem(h_me + off, halves_t))

        @pl.when(off > 1)
        def _():
            pass_on(lax.rem(h_me + off - 1, halves_t))

        return carry

    lax.fori_loop(1, halves_t + 1, step, 0)
    x_rs[last][1]()
    to_col(1.0 / add_up(row_sum, last, n_t))
    send_x(h_me, 1 - l_me).wait_recv()
    total = own_rows(h_me) + from_x[h_me]
    for off in range(1, halves_t):
        h = lax.rem(h_me + off, halves_t)
        send_z(h, h).wait_recv()
        total += from_z[h]
    inv = col[pl.ds(pl.multiple_of(t_me * rows_own, 8), rows_own), :]
    inv = jnp.concatenate([inv] * (feat // LANES), axis=1)
    vel_ref[...] = total * inv - noise_ref[...]

    g_src[3]()
    g_tgt[3]()
    for ops in [x_rp, x_cp] + x_rs + x_cs:
        ops[2]()
    for off in range(1, halves_t):
        h = lax.rem(h_me + off, halves_t)
        send_x(h, 1 - l_me).wait_send()
        send_z(h, h_me).wait_send()
    send_x(h_me, 1 - l_me).wait_send()


def per_device(n_s, n_t, noise, data):
    rows_own, feat = noise.shape
    n_rows, n_cols = rows_own * n_t, data.shape[0]
    rc, cc = n_rows // LANES, n_cols // LANES
    nh, nhs = n_t // 2, n_s // 2
    f32, bf16 = jnp.float32, jnp.bfloat16
    vmem = pltpu.VMEM
    dma = pltpu.SemaphoreType.DMA
    vel, pot = pl.pallas_call(
        functools.partial(kernel, n_s, n_t),
        out_shape=(jax.ShapeDtypeStruct((rows_own, feat), f32), jax.ShapeDtypeStruct((cc, LANES), f32)),
        in_specs=[pl.BlockSpec(memory_space=vmem)] * 2,
        out_specs=(pl.BlockSpec(memory_space=vmem), pl.BlockSpec(memory_space=vmem)),
        scratch_shapes=[
            vmem((n_rows, feat), f32), vmem((feat, n_cols), f32),
            vmem((feat, n_cols), bf16), vmem((feat, n_cols), bf16),
            vmem((n_rows, n_cols), f32), vmem((n_rows, LANES), f32), vmem((n_rows, feat), f32),
            vmem((n_t, 2 * rc, LANES), f32), vmem((n_s, 2 * cc, LANES), f32),
            vmem((ITERS, n_t, rc, LANES), f32), vmem((ITERS - 1, n_s, cc, LANES), f32),
            vmem((nh, rows_own, feat), f32), vmem((nh, rows_own, feat), f32), vmem((nh, rows_own, feat), f32),
            dma((nh,)), dma((nh,)), dma((nh,)), dma((nh,)),
            dma((nhs,)), dma((nhs,)), dma((nhs,)), dma((nhs,)),
            dma((n_t,)), dma((n_t,)), dma((n_s,)), dma((n_s,)),
            dma((ITERS, n_t)), dma((ITERS, n_t)), dma((ITERS - 1, n_s)), dma((ITERS - 1, n_s)),
            dma((nh,)), dma((nh,)), dma((nh,)), dma((nh,)),
        ],
        compiler_params=pltpu.CompilerParams(
            collective_id=0, has_side_effects=True, vmem_limit_bytes=48 * 1024 * 1024),
    )(noise, data)
    return vel, pot.reshape(n_cols)


def solution(mesh):
    return jax.shard_map(
        functools.partial(per_device, mesh.shape["src"], mesh.shape["tgt"]),
        mesh=mesh,
        in_specs=(P(("src", "tgt"), None), P("tgt", "src")),
        out_specs=(P(("src", "tgt"), None), P("tgt")),
        check_vma=False,
    )
```

time: 399 us -> 95.7 us (0.24)
  blocking collectives: 182 us -> 0 us
  waiting for transfers between devices: 133 us -> 0 us
  Pallas kernels: 0 us -> 92.4 us
  other arithmetic: 42.8 us -> 0 us
  matrix products: 27 us -> 0 us
  between operations: 13.9 us -> 0.66 us
    pmax x7 -> x0, blocking collectives: 93.7 us -> none  [the longest x4 76.7 us: row_merge(): top = lax.pmax(local_top, 'tgt')]
    pallas_call x0 -> x1, Pallas kernels: none -> 92.4 us  [per_device(): pl.pallas_call(functools.partial(kernel, n_s, n_t), out_shape=(jax.ShapeD...]
    psum x7 -> x0, blocking collectives: 88.1 us -> none  [the longest x4 68.6 us: row_merge(): total = lax.psum(jnp.sum(jnp.exp(z_tile - top[:, None]), axis=1), 'tgt')]
    all_gather x2 -> x0, waiting for transfers between devices: 68.1 us -> none  [the longest x1 44.8 us: per_device(): source_rows = lax.all_gather(noise, 'tgt', axis=0, tiled=True)]
    reduce_scatter x1 -> x0, waiting for transfers between devices: 63.1 us -> none  [per_device(): lax.psum_scatter(jnp.dot(weight, target_rows, precision=lax.Precision.HIG...]
    dot_general x2 -> x0, matrix products: 27 us -> none  [the longest x1 16.4 us: per_device(): jnp.dot(weight, target_rows, precision=lax.Precision.HIGHEST, preferred_e...]
    reduce_sum x9 -> x0, other arithmetic: 24.9 us -> none  [the longest x4 12.3 us: row_merge(): total = lax.psum(jnp.sum(jnp.exp(z_tile - top[:, None]), axis=1), 'tgt')]
    reduce_max x6 -> x0, other arithmetic: 16.2 us -> none  [the longest x3 8.13 us: row_merge(): local_top = jnp.max(z_tile, axis=1)]
  transfers between devices with their start and end apart: 3 -> 0, of which waited for: 3 -> 0; matrix products, arithmetic and copies ran while one was open for 0% -> 0% of each run, Pallas kernels for 0% -> 0%
where the time goes in v1:
time: 95.7 us; the launch traced here: 95.6 us
  Pallas kernels  92.4 us (97%)
  local copies, waits for them, and re-layouts  2.51 us (3%)
    pallas_call x1, Pallas kernels, per_device(): pl.pallas_call(functools.partial(kernel, n_s, n_t), out_shape=(jax.ShapeD...  92.4 us
    unnamed x5, local copies, waits for them, and re-layouts  2.51 us

profile of v1, /device:TPU:0, one launch (start us, length us, event | category | flops | bytes accessed | tf_op | source)
XLA Modules:
  0.0 95.6 jit_solution(13680851590575105637)
XLA Ops:
  0.6 0.0 copy-start
  0.6 1.2 %copy.4.data_ref = f32[1024,96]{1,0:T(8,128)S(1)} copy(f32[1024,96]{0,1:T(8,128)} %param.3) | data formatting | bytes 786432 | tf_op args[1]
  1.9 0.0 copy-done
  1.9 92.4 %shard_map.41 = (f32[128,384]{1,0:T(8,128)S(1)}, f32[8,128]{1,0:T(8,128)S(1)}) custom-call(f32[128,384]{1,0:T(8,128)S(1)} %copy-done, f32[1024,96]{1,0:T(8,128)S(1)} %copy.4.data_ref), custom_call_target="tpu_custom_call" | custom-call | tf_op jit(solution)/shard_map/pallas_call | solution.py:328
  94.3 0.7 copy.7
  95.0 0.6 copy.8
Async XLA Ops:
  0.6 1.2 %copy-start = (f32[128,384]{1,0:T(8,128)S(1)}, f32[128,384]{1,0:T(8,128)}, u32[]{:S(2)}) copy-start(f32[128,384]{1,0:T(8,128)} %noise_ref.1) | copy-start | bytes 589828

commit v2 on v1

--- a/solution.py
+++ b/solution.py
@@ -22,7 +22,7 @@
 
 def kernel(n_s, n_t, noise_ref, data_ref, vel_ref, pot_ref, src_all, tgt_all, tgt_hi, tgt_lo, tile, col, bary,
            row_pair, col_pair, row_sum, col_sum, from_x, to_z, from_z,
-           src_ss, src_rs, src_fs, src_fr, tgt_ss, tgt_rs, tgt_fs, tgt_fr,
+           src_us, src_ds, src_rs, src_fs, src_fr, tgt_ss, tgt_rs, tgt_fs, tgt_fr,
            rp_s, rp_r, cp_s, cp_r, rs_s, rs_r, cs_s, cs_r, ax_s, ax_r, bz_s, bz_r):
     s_me, t_me = lax.axis_index("src"), lax.axis_index("tgt")
     rows_own, feat = noise_ref.shape
@@ -48,10 +48,6 @@
     src_all[pl.ds(pl.multiple_of(t_me * rows_own, 8), rows_own), :] = noise_ref[...]
     pl.semaphore_wait(barrier, n_t + n_s - 2)
 
-    def remote(ref, where, dst, send, recv, dev):
-        return pltpu.make_async_remote_copy(
-            src_ref=ref.at[where], dst_ref=dst, send_sem=send, recv_sem=recv, device_id=dev, device_id_type=MESH)
-
     def gather_ops(buf, rows, n, me, dev_of, ss, rs, fs, fr):
         hi, lo = me // 2, lax.rem(me, 2)
         nh = n // 2
@@ -96,12 +92,64 @@
 
         return begin, forward, finish, drain
 
-    g_src = gather_ops(src_all, rows_own, n_t, t_me, on_tgt, src_ss, src_rs, src_fs, src_fr)
+    h_me, l_me = t_me // 2, lax.rem(t_me, 2)
+    partner = h_me * 2 + 1 - l_me
+
+    def src_copy(h, low, send, recv, dev):
+        ref = src_all.at[pl.ds(pl.multiple_of((h * 2 + low) * rows_own, 8), rows_own), :]
+        return pltpu.make_async_remote_copy(
+            src_ref=ref, dst_ref=ref, send_sem=send.at[h], recv_sem=recv.at[h],
+            device_id=on_tgt(dev), device_id_type=MESH)
+
+    def up(h):
+        return src_copy(h, l_me, src_us, src_rs, t_me + 2)
+
+    def down(h):
+        return src_copy(h, l_me, src_ds, src_rs, t_me - 2)
+
+    def near(h):
+        return src_copy(h, l_me, src_fs, src_fr, partner)
+
+    def send_on(h, go_up, go_down):
+        if go_up:
+            @pl.when(h_me < halves_t - 1)
+            def _():
+                up(h).start()
+        if go_down:
+            @pl.when(h_me > 0)
+            def _():
+                down(h).start()
+        near(h).start()
+
+    def forward(k):
+        @pl.when(h_me - k >= 0)
+        def _():
+            src_copy(h_me - k, l_me, src_us, src_rs, partner).wait_recv()
+            send_on(h_me - k, True, False)
+
+        @pl.when(h_me + k < halves_t)
+        def _():
+            src_copy(h_me + k, l_me, src_ds, src_rs, partner).wait_recv()
+            send_on(h_me + k, False, True)
+
+    def drain_src():
+        for h in range(halves_t):
+            @pl.when(jnp.logical_and(h <= h_me, h_me < halves_t - 1))
+            def _(h=h):
+                up(h).wait_send()
+
+            @pl.when(jnp.logical_and(h >= h_me, h_me > 0))
+            def _(h=h):
+                down(h).wait_send()
+
+            near(h).wait_send()
+
     g_tgt = gather_ops(tgt_all, feat_own, n_s, s_me, on_src, tgt_ss, tgt_rs, tgt_fs, tgt_fr)
-    g_src[0]()
+    send_on(h_me, True, True)
     g_tgt[0]()
+    forward(1)
     g_tgt[1]()
-    g_src[1]()
+    forward(2)
     g_tgt[2]()
 
     def exchange(buf, n, me, dev_of, ss, rs):
@@ -134,42 +182,58 @@
     t_hi, t_lo = split(tgt_all[...])
     tgt_hi[...] = t_hi
     tgt_lo[...] = t_lo
-    g_src[2]()
-    source = src_all[...]
-    source_sq = jnp.broadcast_to(jnp.sum(source * source, axis=1, keepdims=True), (n_rows, LANES))
-    col[...] = source_sq
-    s_hi, s_lo = split(source)
-    width = 2 * LANES
-
-    def cost_step(k, carry):
-        cols = pl.ds(pl.multiple_of(k * width, width), width)
-        w_hi, w_lo = tgt_hi[:, cols], tgt_lo[:, cols]
-        cross = jnp.dot(s_hi, w_hi, preferred_element_type=f32)
-        cross += jnp.dot(s_hi, w_lo, preferred_element_type=f32)
-        cross += jnp.dot(s_lo, w_hi, preferred_element_type=f32)
-        block = tgt_all[:, cols]
-        target_sq = jnp.sum(block * block, axis=0, keepdims=True)
-        both = jnp.concatenate([col[...], col[...]], axis=1)
-        tile[:, cols] = (both + target_sq - 2.0 * cross) * scale
-        return carry
-
-    lax.fori_loop(0, n_cols // width, cost_step, 0)
+    target_sq = jnp.sum(tgt_all[...] * tgt_all[...], axis=0, keepdims=True)
+    pair = 2 * rows_own
 
     def rows_of(c):
         return slice(c * LANES, (c + 1) * LANES)
 
-    for c in range(row_chunks):
-        top = -tile[rows_of(c), rows_of(0)]
+    def first_row_sums(c):
+        rows = pl.ds(pl.multiple_of(c * LANES, LANES), LANES)
+        top = -tile[rows, rows_of(0)]
         for k in range(1, col_chunks):
-            top = jnp.maximum(top, -tile[rows_of(c), rows_of(k)])
+            top = jnp.maximum(top, -tile[rows, rows_of(k)])
         total = jnp.zeros_like(top)
         for k in range(col_chunks):
-            total += jnp.exp2(-tile[rows_of(c), rows_of(k)] - top)
+            total += jnp.exp2(-tile[rows, rows_of(k)] - top)
         top, total = top.T, total.T
         best = jnp.max(top, axis=0, keepdims=True)
-        row_pair[t_me, c:c + 1, :] = best
-        row_pair[t_me, row_chunks + c:row_chunks + c + 1, :] = jnp.sum(
-            total * jnp.exp2(top - best), axis=0, keepdims=True)
+        row_pair[t_me, pl.ds(c, 1), :] = best
+        row_pair[t_me, pl.ds(row_chunks + c, 1), :] = jnp.sum(total * jnp.exp2(top - best), axis=0, keepdims=True)
+
+    def cost_rows(h):
+        src_copy(h, 1 - l_me, src_fs, src_fr, partner).wait_recv()
+        rows = pl.ds(pl.multiple_of(h * pair, 16), pair)
+        source = src_all[rows, :]
+        source_sq = jnp.sum(source * source, axis=1, keepdims=True)
+        s_hi, s_lo = split(source)
+        cross = jnp.dot(s_hi, tgt_hi[...], preferred_element_type=f32)
+        cross += jnp.dot(s_hi, tgt_lo[...], preferred_element_type=f32)
+        cross += jnp.dot(s_lo, tgt_hi[...], preferred_element_type=f32)
+        tile[rows, :] = (source_sq + target_sq - 2.0 * cross) * scale
+        if pair % LANES == 0:
+            for c in range(pair // LANES):
+                first_row_sums(h * (pair // LANES) + c)
+
+    def cost_step(index, carry):
+        k, side = index // 2, lax.rem(index, 2)
+        h = h_me + (2 * side - 1) * k
+
+        @pl.when(jnp.logical_and(jnp.logical_and(h >= 0, h < halves_t), k + side > 0))
+        def _():
+            cost_rows(h)
+
+        @pl.when(index == 1)
+        def _():
+            for k in range(3, halves_t):
+                forward(k)
+
+        return carry
+
+    lax.fori_loop(1, 2 * halves_t, cost_step, 0)
+    if pair % LANES != 0:
+        for c in range(row_chunks):
+            first_row_sums(c)
     x_rp[0]()
     x_rp[1]()
 
@@ -253,8 +317,6 @@
         tgt_hi[:, rows_of(k)] = t_hi
         tgt_lo[:, rows_of(k)] = t_lo
 
-    h_me, l_me = t_me // 2, lax.rem(t_me, 2)
-    pair = 2 * rows_own
     dims = (((1,), (1,)), ((), ()))
 
     def send_x(h, lo):
@@ -306,7 +368,7 @@
     inv = jnp.concatenate([inv] * (feat // LANES), axis=1)
     vel_ref[...] = total * inv - noise_ref[...]
 
-    g_src[3]()
+    drain_src()
     g_tgt[3]()
     for ops in [x_rp, x_cp] + x_rs + x_cs:
         ops[2]()
@@ -337,7 +399,7 @@
             vmem((n_t, 2 * rc, LANES), f32), vmem((n_s, 2 * cc, LANES), f32),
             vmem((ITERS, n_t, rc, LANES), f32), vmem((ITERS - 1, n_s, cc, LANES), f32),
             vmem((nh, rows_own, feat), f32), vmem((nh, rows_own, feat), f32), vmem((nh, rows_own, feat), f32),
-            dma((nh,)), dma((nh,)), dma((nh,)), dma((nh,)),
+            dma((nh,)), dma((nh,)), dma((nh,)), dma((nh,)), dma((nh,)),
             dma((nhs,)), dma((nhs,)), dma((nhs,)), dma((nhs,)),
             dma((n_t,)), dma((n_t,)), dma((n_s,)), dma((n_s,)),
             dma((ITERS, n_t)), dma((ITERS, n_t)), dma((ITERS - 1, n_s)), dma((ITERS - 1, n_s)),

time: 95.7 us -> 80.8 us (0.84)
  Pallas kernels: 92.4 us -> 77.5 us
    pallas_call x1, Pallas kernels: 92.4 us -> 77.5 us  [per_device(): pl.pallas_call(functools.partial(kernel, n_s, n_t), out_shape=(jax.ShapeD...]
where the time goes in v2:
time: 80.8 us; the launch traced here: 80.7 us
  Pallas kernels  77.5 us (96%)
  local copies, waits for them, and re-layouts  2.51 us (3%)
    pallas_call x1, Pallas kernels, per_device(): pl.pallas_call(functools.partial(kernel, n_s, n_t), out_shape=(jax.ShapeD...  77.5 us
    unnamed x5, local copies, waits for them, and re-layouts  2.51 us

profile of v2, /device:TPU:0, one launch (start us, length us, event | category | flops | bytes accessed | tf_op | source)
XLA Modules:
  0.0 80.7 jit_solution(7640653324788520398)
XLA Ops:
  0.6 0.0 copy-start
  0.6 1.2 %copy.4.data_ref = f32[1024,96]{1,0:T(8,128)S(1)} copy(f32[1024,96]{0,1:T(8,128)} %param.3) | data formatting | bytes 786432 | tf_op args[1]
  1.9 0.0 copy-done
  1.9 77.5 %shard_map.41 = (f32[128,384]{1,0:T(8,128)S(1)}, f32[8,128]{1,0:T(8,128)S(1)}) custom-call(f32[128,384]{1,0:T(8,128)S(1)} %copy-done, f32[1024,96]{1,0:T(8,128)S(1)} %copy.4.data_ref), custom_call_target="tpu_custom_call" | custom-call | tf_op jit(solution)/shard_map/pallas_call | solution.py:390
  79.4 0.7 copy.7
  80.1 0.6 copy.8
Async XLA Ops:
  0.6 1.2 %copy-start = (f32[128,384]{1,0:T(8,128)S(1)}, f32[128,384]{1,0:T(8,128)}, u32[]{:S(2)}) copy-start(f32[128,384]{1,0:T(8,128)} %noise_ref.1) | copy-start | bytes 589828

commit v3 on v2

--- a/solution.py
+++ b/solution.py
@@ -26,7 +26,7 @@
            rp_s, rp_r, cp_s, cp_r, rs_s, rs_r, cs_s, cs_r, ax_s, ax_r, bz_s, bz_r):
     s_me, t_me = lax.axis_index("src"), lax.axis_index("tgt")
     rows_own, feat = noise_ref.shape
-    feat_own = data_ref.shape[1]
+    feat_own = data_ref.shape[0]
     n_rows, n_cols = tile.shape
     row_chunks, col_chunks = n_rows // LANES, n_cols // LANES
     src_total, tgt_total = n_rows * n_s, n_cols * n_t
@@ -44,7 +44,7 @@
         pl.semaphore_signal(barrier, 1, device_id=on_tgt(lax.rem(t_me + off, n_t)), device_id_type=MESH)
     for off in range(1, n_s):
         pl.semaphore_signal(barrier, 1, device_id=on_src(lax.rem(s_me + off, n_s)), device_id_type=MESH)
-    tgt_all[pl.ds(pl.multiple_of(s_me * feat_own, 8), feat_own), :] = data_ref[...].T
+    tgt_all[pl.ds(pl.multiple_of(s_me * feat_own, 8), feat_own), :] = data_ref[...]
     src_all[pl.ds(pl.multiple_of(t_me * rows_own, 8), rows_own), :] = noise_ref[...]
     pl.semaphore_wait(barrier, n_t + n_s - 2)
 
@@ -310,8 +310,6 @@
     pot_ref[...] = EPS * (g_first * math.log(2.0) + jnp.log(beta))
 
     last = ITERS - 1
-    row_products(last, b)
-    x_rs[last][0]()
     for k in range(col_chunks):
         t_hi, t_lo = split(tgt_all[:, rows_of(k)] * b[k:k + 1, :])
         tgt_hi[:, rows_of(k)] = t_hi
@@ -333,13 +331,17 @@
         return bary[pl.ds(pl.multiple_of((h * 2 + l_me) * rows_own, 8), rows_own), :]
 
     def compute(h):
-        rows = pl.ds(pl.multiple_of(h * pair, 16), pair)
+        product(h, 1 - l_me)
+        send_x(h, 1 - l_me).start()
+        product(h, l_me)
+
+    def product(h, lo):
+        rows = pl.ds(pl.multiple_of((h * 2 + lo) * rows_own, 16), rows_own)
         e_hi, e_lo = split(tile[rows, :])
         out = lax.dot_general(e_hi, tgt_hi[...], dims, preferred_element_type=f32)
         out += lax.dot_general(e_hi, tgt_lo[...], dims, preferred_element_type=f32)
         out += lax.dot_general(e_lo, tgt_hi[...], dims, preferred_element_type=f32)
         bary[rows, :] = out
-        send_x(h, 1 - l_me).start()
 
     def pass_on(h):
         send_x(h, 1 - l_me).wait_recv()
@@ -348,6 +350,11 @@
 
     def step(off, carry):
         compute(lax.rem(h_me + off, halves_t))
+
+        @pl.when(off == 1)
+        def _():
+            row_products(last, b)
+            x_rs[last][0]()
 
         @pl.when(off > 1)
         def _():
@@ -407,7 +414,7 @@
         ],
         compiler_params=pltpu.CompilerParams(
             collective_id=0, has_side_effects=True, vmem_limit_bytes=48 * 1024 * 1024),
-    )(noise, data)
+    )(noise, data.T)
     return vel, pot.reshape(n_cols)
 
 

time: 80.8 us -> 81.1 us (level)
    unnamed x5 -> x6, local copies, waits for them, and re-layouts: 2.51 us -> 3.19 us
where the time goes in v3:
time: 81.1 us; the launch traced here: 80.9 us
  Pallas kernels  77.1 us (95%)
  local copies, waits for them, and re-layouts  3.19 us (4%)
    pallas_call x1, Pallas kernels, per_device(): pl.pallas_call(functools.partial(kernel, n_s, n_t), out_shape=(jax.ShapeD...  77.1 us
    unnamed x6, local copies, waits for them, and re-layouts  3.19 us

profile of v3, /device:TPU:0, one launch (start us, length us, event | category | flops | bytes accessed | tf_op | source)
XLA Modules:
  0.0 80.9 jit_solution(12482969004772013238)
XLA Ops:
  0.6 0.0 copy-start
  0.6 1.0 %copy-done = f32[1024,96]{0,1:T(8,128)S(1)} copy-done((f32[1024,96]{0,1:T(8,128)S(1)}, f32[1024,96]{0,1:T(8,128)}, u32[]{:S(2)}) %copy-start) | copy-done | bytes 393240
  1.6 0.0 copy-start.1
  1.6 0.9 %copy-done.1 = f32[128,384]{1,0:T(8,128)S(1)} copy-done((f32[128,384]{1,0:T(8,128)S(1)}, f32[128,384]{1,0:T(8,128)}, u32[]{:S(2)}) %copy-start.1) | copy-done | bytes 196632
  2.6 77.1 %shard_map.41 = (f32[128,384]{1,0:T(8,128)S(1)}, f32[8,128]{1,0:T(8,128)S(1)}) custom-call(f32[128,384]{1,0:T(8,128)S(1)} %copy-done.1, f32[96,1024]{1,0:T(8,128)S(1)} %bitcast.2), custom_call_target="tpu_custom_call" | custom-call | tf_op jit(solution)/shard_map/pallas_call | solution.py:397
  79.7 0.7 copy.6
  80.3 0.6 copy.7
Async XLA Ops:
  0.6 1.0 %copy-start = (f32[1024,96]{0,1:T(8,128)S(1)}, f32[1024,96]{0,1:T(8,128)}, u32[]{:S(2)}) copy-start(f32[1024,96]{0,1:T(8,128)} %param.3) | copy-start | bytes 1179652
  1.6 0.9 %copy-start.1 = (f32[128,384]{1,0:T(8,128)S(1)}, f32[128,384]{1,0:T(8,128)}, u32[]{:S(2)}) copy-start(f32[128,384]{1,0:T(8,128)} %noise_ref.1) | copy-start | bytes 589828

commit v4 on v3

--- a/solution.py
+++ b/solution.py
@@ -331,12 +331,11 @@
         return bary[pl.ds(pl.multiple_of((h * 2 + l_me) * rows_own, 8), rows_own), :]
 
     def compute(h):
-        product(h, 1 - l_me)
+        product(h, 0)
         send_x(h, 1 - l_me).start()
-        product(h, l_me)
 
     def product(h, lo):
-        rows = pl.ds(pl.multiple_of((h * 2 + lo) * rows_own, 16), rows_own)
+        rows = pl.ds(pl.multiple_of(h * pair, 16), pair)
         e_hi, e_lo = split(tile[rows, :])
         out = lax.dot_general(e_hi, tgt_hi[...], dims, preferred_element_type=f32)
         out += lax.dot_general(e_hi, tgt_lo[...], dims, preferred_element_type=f32)
@@ -348,21 +347,14 @@
         to_z[h] = own_rows(h) + from_x[h]
         send_z(h, h_me).start()
 
-    def step(off, carry):
+    order = sorted(range(1, halves_t), key=lambda off: abs(2 * off - halves_t)) + [halves_t]
+    for at, off in enumerate(order):
         compute(lax.rem(h_me + off, halves_t))
-
-        @pl.when(off == 1)
-        def _():
+        if at == 0:
             row_products(last, b)
             x_rs[last][0]()
-
-        @pl.when(off > 1)
-        def _():
-            pass_on(lax.rem(h_me + off - 1, halves_t))
-
-        return carry
-
-    lax.fori_loop(1, halves_t + 1, step, 0)
+        else:
+            pass_on(lax.rem(h_me + order[at - 1], halves_t))
     x_rs[last][1]()
     to_col(1.0 / add_up(row_sum, last, n_t))
     send_x(h_me, 1 - l_me).wait_recv()

time: 81.1 us -> 81.3 us (level)
  no operation moved by 1% of the time
where the time goes in v4:
time: 81.3 us; the launch traced here: 81.1 us
  Pallas kernels  77.3 us (95%)
  local copies, waits for them, and re-layouts  3.19 us (4%)
    pallas_call x1, Pallas kernels, per_device(): pl.pallas_call(functools.partial(kernel, n_s, n_t), out_shape=(jax.ShapeD...  77.3 us
    unnamed x6, local copies, waits for them, and re-layouts  3.19 us

profile of v4, /device:TPU:0, one launch (start us, length us, event | category | flops | bytes accessed | tf_op | source)
XLA Modules:
  0.0 81.1 jit_solution(12437616823769254563)
XLA Ops:
  0.6 0.0 copy-start
  0.6 1.0 %copy-done = f32[1024,96]{0,1:T(8,128)S(1)} copy-done((f32[1024,96]{0,1:T(8,128)S(1)}, f32[1024,96]{0,1:T(8,128)}, u32[]{:S(2)}) %copy-start) | copy-done | bytes 393240
  1.6 0.0 copy-start.1
  1.6 0.9 %copy-done.1 = f32[128,384]{1,0:T(8,128)S(1)} copy-done((f32[128,384]{1,0:T(8,128)S(1)}, f32[128,384]{1,0:T(8,128)}, u32[]{:S(2)}) %copy-start.1) | copy-done | bytes 196632
  2.6 77.3 %shard_map.41 = (f32[128,384]{1,0:T(8,128)S(1)}, f32[8,128]{1,0:T(8,128)S(1)}) custom-call(f32[128,384]{1,0:T(8,128)S(1)} %copy-done.1, f32[96,1024]{1,0:T(8,128)S(1)} %bitcast.2), custom_call_target="tpu_custom_call" | custom-call | tf_op jit(solution)/shard_map/pallas_call | solution.py:389
  79.8 0.7 copy.6
  80.5 0.6 copy.7
Async XLA Ops:
  0.6 1.0 %copy-start = (f32[1024,96]{0,1:T(8,128)S(1)}, f32[1024,96]{0,1:T(8,128)}, u32[]{:S(2)}) copy-start(f32[1024,96]{0,1:T(8,128)} %param.3) | copy-start | bytes 1179652
  1.6 0.9 %copy-start.1 = (f32[128,384]{1,0:T(8,128)S(1)}, f32[128,384]{1,0:T(8,128)}, u32[]{:S(2)}) copy-start(f32[128,384]{1,0:T(8,128)} %noise_ref.1) | copy-start | bytes 589828
